TPU v7x, 32 devices: a whole 2x2x4 slice. The times are simulated.
32 devices in a mesh: dp: 8 (over z, x), head: 4 (over y, core).
Axes of the slice: x: 2, y: 2, z: 4, core: 2. Of those that a mesh axis runs over, the one named last changes fastest.
Arguments:
- grads: bfloat16 [8, 2, 512, 16384], P('dp', None, None, 'head'), may hold values from -6 to 6
- owners: int32 [2], replicated, may hold values from 0 to 7, as said below
Outputs:
- updates: bfloat16 [2, 512, 16384], P(None, 'dp', 'head')
- owned: bfloat16 [8, 512, 16384], P('dp', None, 'head')
Inputs may be any that keep to these rules, and one draw needn't show every extreme that they name: The owners are distinct ranks of the data axis: each rank owns at most one of the 2 layers.
All inputs are finite; a program needn't handle non-finite values.
Results may differ from a plain program's by a relative error of at most 0.014.
Values may be sent and summed in bfloat16 or wider, within the bound.
A program may use at most 64 MiB of HBM per device.

v0:
```python
import math

import jax
import jax.numpy as jnp
from jax import lax
from jax.sharding import PartitionSpec as P

R = 512
HEADS = 64
HDIM = 256
ITERS = 2


COEF_A = 3.4445
COEF_B = -4.775
COEF_C = 2.0315
EPS = 1e-07


def orthogonalize(start, sum_gram):
    iterate = start
    stepped = None
    for step_index in range(ITERS):
        gram_part = sum_gram(
            jnp.einsum("...rc,...sc->...rs", iterate, iterate, preferred_element_type=jnp.float32)
        )
        if step_index == 0:
            squares = jnp.trace(gram_part, axis1=-2, axis2=-1)
            inverse = lax.rsqrt(squares + EPS)[..., None, None]
            gram = gram_part * (inverse * inverse)
        else:
            gram = gram_part
        polynomial = (
            COEF_B * gram + COEF_C * jnp.matmul(gram, gram, precision=lax.Precision.HIGHEST)
        ).astype(jnp.bfloat16)
        stepped = COEF_A * iterate.astype(jnp.float32) + jnp.einsum(
            "...rs,...sc->...rc", polynomial, iterate, preferred_element_type=jnp.float32
        )
        if step_index == 0:
            stepped = inverse * stepped
        if step_index + 1 < ITERS:
            iterate = stepped.astype(jnp.bfloat16)
    return (0.2 * math.sqrt(max(R, HEADS * HDIM)) * stepped).astype(jnp.bfloat16)


def per_device(grads, owners):
    partial_value = grads[0].astype(jnp.float32)
    summed = lax.psum_scatter(
        partial_value.astype(jnp.bfloat16), "dp", scatter_dimension=2, tiled=True
    )
    own_rank = lax.axis_index("dp")
    chosen = (owners == own_rank).astype(jnp.bfloat16)
    row_count = R // lax.axis_size("dp")
    row_start = own_rank * row_count

    def wide_total(gram_part):
        return lax.psum(gram_part, ("dp", "head"))

    spread = orthogonalize(summed, wide_total)
    every_layer = lax.all_gather(spread, "dp", axis=2, tiled=True)
    updates = lax.dynamic_slice_in_dim(every_layer, row_start, row_count, 1)
    owned = jnp.einsum("l,lrc->rc", chosen, every_layer, preferred_element_type=jnp.float32).astype(
        jnp.bfloat16
    )[None]
    return (updates, owned)


def solution(mesh):
    in_specs = (P("dp", None, None, "head"), P())
    out_specs = (P(None, "dp", "head"), P("dp", None, "head"))
    return jax.shard_map(
        per_device, mesh=mesh, in_specs=in_specs, out_specs=out_specs, check_vma=False
    )
```

profile of v0, /device:TPU:0, one launch (start us, length us, event | category | flops | bytes accessed | tf_op | source)
XLA Modules:
  0.0 608.6 jit_solution(6817601352141066874)
XLA Ops:
  7.2 0.0 reduce-scatter.2.cloned.1.call-start
  7.2 0.7 reduce-scatter.2.cloned.1.call-update
  7.9 0.0 all-reduce.3.cloned.1.call-start
  7.9 155.8 %reduce-scatter.2.cloned.1.call-done = bf16[2,512,512]{2,1,0:T(8,128)(2,1)} async-done(((bf16[2,512,4096]{2,1,0:T(8,128)(2,1)}), bf16[2,512,512]{2,1,0:T(8,128)(2,1)}) %reduce-scatter.2.cloned.1.call-update) | async-done | bytes 1048592 | tf_op jit(solution)/shard_map/reduce_scatter | solution.py:48
  163.7 3.7 fusion.10
  167.4 0.0 all-reduce.3.cloned.1.call-update
  167.4 0.0 all-reduce.5.cloned.1.call-start
  167.5 0.1 iota_compare_fusion
  167.6 135.8 %all-reduce.3.cloned.1.call-done = f32[2,512,512]{2,1,0:T(8,128)} async-done(((f32[2,512,512]{2,1,0:T(8,128)}), f32[2,512,512]{2,1,0:T(8,128)}) %all-reduce.3.cloned.1.call-update) | async-done | bytes 2097168 | tf_op jit(solution)/shard_map/psum | solution.py:57
  303.3 0.0 copy-start.1
  303.3 2.2 select_reduce_fusion
  305.5 0.0 copy-done.1
  305.6 0.0 copy-start
  305.6 3.9 add_convert_fusion.1
  309.5 0.0 copy-done
  309.5 0.7 multiply_convert_fusion.1
  310.2 2.1 fusion.11
  312.3 0.0 all-reduce.5.cloned.1.call-update
  312.3 0.0 all-gather.2.cloned.1.call-start
  312.3 132.7 %all-reduce.5.cloned.1.call-done = f32[2,512,512]{2,1,0:T(8,128)} async-done(((f32[2,512,512]{2,1,0:T(8,128)}), f32[2,512,512]{2,1,0:T(8,128)}) %all-reduce.5.cloned.1.call-update) | async-done | bytes 2097168 | tf_op jit(solution)/shard_map/psum | solution.py:57
  445.1 6.5 %add_convert_fusion = bf16[2,512,512]{2,1,0:T(8,128)(2,1)S(1)} fusion(f32[2,512,512]{2,1,0:T(8,128)} %all-reduce.5.cloned.1.call-done), kind=kOutput, calls=%fused_computation.5 | convolution fusion | flops 3223322624 | bytes 3145728 | tf_op jit(solution)/shard_map/dot_general | solution.py:34
  451.5 0.0 copy-start.2
  451.6 1.7 multiply_convert_fusion
  453.3 0.0 all-gather.2.cloned.1.call-update
  453.3 124.4 %all-gather.2.cloned.1.call-done = bf16[2,512,4096]{2,1,0:T(8,128)(2,1)} async-done(((bf16[2,512,512]{2,1,0:T(8,128)(2,1)}), bf16[2,512,4096]{2,1,0:T(8,128)(2,1)}) %all-gather.2.cloned.1.call-update) | async-done | bytes 8388624 | tf_op jit(solution)/shard_map/all_gather | solution.py:60
  577.7 0.0 copy-done.2
  577.7 15.3 %fusion = bf16[1,512,4096]{2,0,1:T(2,128)(2,1)S(1)} fusion(bf16[2,512,4096]{2,1,0:T(8,128)(2,1)} %all-gather.2.cloned.1.call-done, s32[2]{0:T(128)S(1)} %copy-done.2, s32[]{:T(128)S(6)} %axis_index.15), kind=kOutput, calls=%fused_computation.1 | convolution fusion | flops 8388610 | bytes 12582924 | tf_op jit(solution)/shard_map/l,lrc->rc/dot_general | solution.py:62
  593.0 6.8 %copy.11 = bf16[1,512,4096]{2,1,0:T(8,128)(2,1)} copy(bf16[1,512,4096]{2,0,1:T(2,128)(2,1)S(1)} %fusion) | data formatting | bytes 8388608 | tf_op jit(solution)/shard_map/l,lrc->rc/dot_general | solution.py:62
  599.8 2.3 constant_dynamic-slice_fusion
  (1 shorter events, 0.0 us)
Async XLA Ops:
  7.2 156.6 %reduce-scatter.2.cloned.1.call-start = ((), (), s32[]{:S(2)}) async-start(), calls=%async_computation.1 | async-start | bytes 9437184 | tf_op jit(solution)/shard_map/reduce_scatter | solution.py:48
  7.9 295.4 %all-reduce.3.cloned.1.call-start = ((), (), s32[]{:S(2)}) async-start(), calls=%async_computation.2 | async-start | bytes 4194304 | tf_op jit(solution)/shard_map/psum | solution.py:57
  167.4 277.7 %all-reduce.5.cloned.1.call-start = ((), (), s32[]{:S(2)}) async-start(), calls=%async_computation.3 | async-start | bytes 4194304 | tf_op jit(solution)/shard_map/psum | solution.py:57
  303.3 2.2 copy-start.1
  305.6 3.9 copy-start
  312.3 265.4 %all-gather.2.cloned.1.call-start = ((), (), s32[]{:S(2)}) async-start(), calls=%async_computation.4 | async-start | bytes 9437184 | tf_op jit(solution)/shard_map/all_gather | solution.py:60
  451.5 126.2 %copy-start.2 = (s32[2]{0:T(128)S(1)}, s32[2]{0:T(128)}, u32[]{:S(2)}) copy-start(s32[2]{0:T(128)} %param.3) | copy-start | bytes 28
Sparse Core Ops, SparseCore 0:
  11.6 152.0 reduce-scatter.1
  170.5 132.7 all-reduce.2
  312.4 132.6 all-reduce.4
  453.4 124.2 all-gather.1
where the time goes:
time: 609 us
  waiting for transfers between devices  549 us (90%)
  matrix products  33.8 us (6%)
  between operations  13.8 us (2%)
  local copies, waits for them, and re-layouts  9.13 us (1%)
    psum x2, waiting for transfers between devices, wide_total(): return lax.psum(gram_part, ('dp', 'head'))  269 us
    reduce_scatter x1, waiting for transfers between devices, per_device(): lax.psum_scatter(partial_value.astype(jnp.bfloat16), 'dp', scatter_dimens...  156 us
    all_gather x1, waiting for transfers between devices, per_device(): every_layer = lax.all_gather(spread, 'dp', axis=2, tiled=True)  124 us
    dot_general x1, matrix products, per_device(): jnp.einsum('l,lrc->rc', chosen, every_layer, preferred_element_type=jnp.f...  15.3 us
  transfers between devices with their start and end apart: 4, of which 4 were waited for; matrix products, arithmetic and copies ran while one was open for 0% of the time, Pallas kernels for 0%

commit v1 on v0

v1 whole, which is shorter than its diff:
```python
import functools
import math

import jax
import jax.numpy as jnp
from jax import lax
from jax.experimental import pallas as pl
from jax.experimental.pallas import tpu as pltpu
from jax.sharding import PartitionSpec as P

COEF_A = 3.4445
COEF_B = -4.775
COEF_C = 2.0315
EPS = 1e-07
TILE = 512
START_ROUND = 5
MESH = pl.DeviceIdType.MESH
F32 = jnp.float32
BF16 = jnp.bfloat16


def add_rows(dst, terms, rows):
    step = 16

    @pl.loop(0, rows // step)
    def _(index):
        at = pl.ds(pl.multiple_of(index * step, step), step)
        total = terms[0][at, :].astype(F32)
        for term in terms[1:]:
            total = total + term[at, :].astype(F32)
        dst[at, :] = total.astype(BF16)


def remote(src, dst, send, recv, device):
    return pltpu.make_async_remote_copy(
        src_ref=src, dst_ref=dst, send_sem=send, recv_sem=recv, device_id=device, device_id_type=MESH
    )


class Line:
    def __init__(self, size, place, device):
        self.size, self.place, self.device = size, place, device

    def left(self):
        return self.device(self.place - 1)

    def right(self):
        return self.device(self.place + 1)


def reduce_scatter(line, view, out, rows, slots, send, recv, drain):
    n, i = line.size, line.place

    def receive(slot):
        remote(slots.at[slot], slots.at[slot], send.at[0, 0], recv.at[slot], line.device(i)).wait_recv()

    def rightward(t):
        copy = remote(view(t), slots.at[t], send.at[0, t], recv.at[t], line.right())
        if t > 1:
            @pl.when((i > 0) & (i < t))
            def _():
                receive(t)
                add_rows(view(t), [view(t), slots.at[t]], rows)

        pl.when(i < t)(copy.start)
        drain.append((i < t, copy))

    def leftward(t):
        slot = jnp.where(i - 1 == t, n, t)
        copy = remote(view(t), slots.at[slot], send.at[1, t], recv.at[slot], line.left())
        if t < n - 2:
            @pl.when((i > t) & (i < n - 1))
            def _():
                receive(t)
                add_rows(view(t), [view(t), slots.at[t]], rows)

        pl.when(i > t)(copy.start)
        drain.append((i > t, copy))

    for step in range(n - 1):
        rightward(n - 1 - step)
        yield
        leftward(step)
        yield

    @pl.when(i == 0)
    def _():
        receive(n)
        add_rows(out, [view(i), slots.at[n]], rows)

    @pl.when(i == n - 1)
    def _():
        receive(i)
        add_rows(out, [view(i), slots.at[i]], rows)

    if n > 2:
        @pl.when((i > 0) & (i < n - 1))
        def _():
            receive(i)
            receive(n)
            add_rows(out, [view(i), slots.at[i], slots.at[n]], rows)
    yield


def all_gather(line, view, send, recv, drain):
    n, i = line.size, line.place

    def move(way, step):
        t = i - step if way == 0 else i + step
        there = t >= 0 if way == 0 else t <= n - 1
        passes = there & (i < n - 1 if way == 0 else i > 0)
        target = line.right() if way == 0 else line.left()
        part = jnp.clip(t, 0, n - 1)
        copy = remote(view(part), view(part), send.at[way, step], recv.at[part], target)
        if step > 0:
            pl.when(there)(copy.wait_recv)
        if step < n - 1:
            pl.when(passes)(copy.start)
            drain.append((passes, copy))

    for step in range(n):
        move(0, step)
        move(1, step)
        yield


def spread_rows(index, rows):
    return pl.ds(pl.multiple_of(index * rows, rows), rows)


def kernel(sizes, *refs):
    z_size, x_size, y_size, rank, wide, wide_b, wide_total = sizes
    n_dp = z_size * x_size
    refs = list(refs)
    take = lambda count: [refs.pop(0) for _ in range(count)]
    grads, chosen, updates, owned = take(4)
    acc, fin = take(2), take(2)
    slots_a, slots_b = take(2), take(2)
    raw, half_in, by_y, full, m0, t0, g1, dmat, outs = take(9)
    load_sem = take(1)[0]
    rs_send, rs_recv = take(4), take(4)
    ag_send, ag_recv = take(4), take(4)
    core_send, core_recv, y_send, y_recv = take(4)

    me, head = lax.axis_index("dp"), lax.axis_index("head")
    z, x = me // x_size, me % x_size
    y, core = head // 2, head % 2
    line_x = Line(x_size, x, lambda place: (z * x_size + place, head))
    line_z = Line(z_size, z, lambda place: (place * x_size + x, head))
    sibling = (me, y * 2 + 1 - core)

    loads = {}
    for layer in range(2):
        for job, (start, width) in enumerate(((0, wide), (wide, wide_b))):
            loads[layer, job] = pltpu.make_async_copy(
                grads.at[0, layer, :, pl.ds(start, width)], acc[job].at[layer], load_sem.at[layer, job]
            )
            loads[layer, job].start()

    barrier = pltpu.get_barrier_semaphore()
    greet = [(z > 0, line_z.left()), (z < z_size - 1, line_z.right())]
    greet += [(x > 0, line_x.left()), (x < x_size - 1, line_x.right())]
    for near, device in greet:
        pl.when(near)(
            functools.partial(
                pl.semaphore_signal, barrier, inc=1, device_id=device, device_id_type=MESH
            )
        )
    pl.semaphore_signal(barrier, inc=1, device_id=sibling, device_id_type=MESH)
    peers = [(me, lax.rem(y + step, y_size) * 2 + core) for step in range(1, y_size)]
    for peer in peers:
        pl.semaphore_signal(barrier, inc=1, device_id=peer, device_id_type=MESH)
    count = jnp.int32(y_size)
    for near, _ in greet:
        count = count + near.astype(jnp.int32)
    pl.semaphore_wait(barrier, count)

    drain = []

    def chain(layer, job):
        first, second = (line_x, line_z) if job == 0 else (line_z, line_x)
        slots1, slots2 = slots_a if job == 0 else slots_b
        big, small = rank // first.size, rank // n_dp
        a, f = acc[job].at[layer], fin[job].at[layer]
        base = first.place * big

        def small_rows(t):
            return pl.ds(pl.multiple_of(base + t * small, small), small)

        loads[layer, job].wait()
        k = 2 * job
        yield from reduce_scatter(
            first, lambda t: a.at[spread_rows(t, big), :], a.at[spread_rows(first.place, big), :], big,
            slots1.at[layer], rs_send[k].at[layer], rs_recv[k].at[layer], drain,
        )
        yield from reduce_scatter(
            second, lambda t: a.at[small_rows(t), :], f.at[small_rows(second.place), :], small,
            slots2.at[layer], rs_send[k + 1].at[layer], rs_recv[k + 1].at[layer], drain,
        )
        yield from all_gather(
            second, lambda t: f.at[small_rows(t), :], ag_send[k + 1].at[layer], ag_recv[k + 1].at[layer], drain
        )
        yield from all_gather(
            first, lambda t: f.at[spread_rows(t, big), :], ag_send[k].at[layer], ag_recv[k].at[layer], drain
        )

    def gram_of(layer, job, width):
        @pl.loop(0, width // TILE)
        def _(index):
            block = fin[job][layer, :, pl.ds(pl.multiple_of(index * TILE, TILE), TILE)]
            raw[layer] += lax.dot_general(
                block, block, (((1,), (1,)), ((), ())), preferred_element_type=F32
            )

    def product(left, right, finish):
        step = 128

        @pl.loop(0, rank // step)
        def _(index):
            at = pl.ds(pl.multiple_of(index * step, step), step)
            finish(at, jnp.dot(left[at, :], right[...], precision=lax.Precision.HIGHEST,
                               preferred_element_type=F32), index * step)

    def eye(start):
        rows = lax.broadcasted_iota(jnp.int32, (128, rank), 0) + start
        return rows == lax.broadcasted_iota(jnp.int32, (128, rank), 1)

    def post(layer):
        raw[layer] = jnp.zeros((rank, rank), F32)
        gram_of(layer, 0, wide)
        yield
        gram_of(layer, 1, wide_b)
        half = rank // 2
        mine, other = spread_rows(core, half), spread_rows(1 - core, half)
        give = remote(raw.at[layer, other, :], half_in.at[layer], core_send.at[layer, 0],
                      core_recv.at[layer, 0], sibling)
        give.start()
        yield
        give.wait_recv()
        by_y[layer, y] = raw[layer, mine, :] + half_in[layer]
        sends = []
        for step, peer in enumerate(peers):
            copy = remote(by_y.at[layer, y], by_y.at[layer, y], y_send.at[layer, step],
                          y_recv.at[layer, y], peer)
            copy.start()
            sends.append(copy)
        yield
        yield
        for step in range(1, y_size):
            source = lax.rem(y + step, y_size)
            remote(by_y.at[layer, source], by_y.at[layer, source], y_send.at[layer, 0],
                   y_recv.at[layer, source], sibling).wait_recv()
        total = by_y[layer, 0]
        for place in range(1, y_size):
            total = total + by_y[layer, place]
        full[layer, mine, :] = total
        share = remote(full.at[layer, mine, :], full.at[layer, mine, :], core_send.at[layer, 1],
                       core_recv.at[layer, 1], sibling)
        share.start()
        give.wait_send()
        for copy in sends:
            copy.wait_send()
        yield
        share.wait_recv()
        share.wait_send()
        raws = full[layer]
        on_diagonal = lax.broadcasted_iota(jnp.int32, (rank, rank), 0) == lax.broadcasted_iota(
            jnp.int32, (rank, rank), 1)
        squares = jnp.sum(jnp.where(on_diagonal, raws, 0.0), axis=0, keepdims=True)
        squares = jnp.sum(squares, axis=1, keepdims=True)
        inverse = lax.rsqrt(squares + EPS)
        gram = raw.at[layer]
        gram[...] = raws * (inverse * inverse)

        def to_m0(at, value, start):
            m0[at, :] = COEF_B * gram[at, :] + COEF_C * value + jnp.where(eye(start), COEF_A, 0.0)

        product(gram, gram, to_m0)
        yield

        def to_t0(at, value, start):
            t0[at, :] = value

        product(m0, gram, to_t0)
        yield

        def to_g1(at, value, start):
            g1[at, :] = value

        product(t0, m0, to_g1)
        yield

        def to_m1(at, value, start):
            t0[at, :] = COEF_B * g1[at, :] + COEF_C * value

        product(g1, g1, to_m1)
        yield
        scale = inverse * (0.2 * math.sqrt(max(rank, wide_total)))

        def to_d(at, value, start):
            rest = value + COEF_A * (m0[at, :] - jnp.where(eye(start), COEF_A, 0.0))
            dmat[at, :] = (scale * rest).astype(BF16)

        product(t0, m0, to_d)
        yield
        weight = chosen[layer]
        rows = rank // n_dp
        diagonal = scale * (COEF_A * COEF_A)
        for job, (start, width) in enumerate(((0, wide), (wide, wide_b))):
            @pl.loop(0, width // TILE)
            def _(index):
                offset = pl.multiple_of(index * TILE, TILE)
                block = fin[job][layer, :, pl.ds(offset, TILE)]
                value = jnp.dot(dmat[...], block, preferred_element_type=F32)
                value = (value + diagonal * block.astype(F32)).astype(BF16)
                outs[...] = value
                at = pl.ds(pl.multiple_of(start + offset, TILE), TILE)
                updates[layer, :, at] = outs[spread_rows(me, rows), :]
                picked = weight * value.astype(F32)
                if layer > 0:
                    picked = picked + owned[0, :, at].astype(F32)
                owned[0, :, at] = picked.astype(BF16)

            yield

    def whole_layer(layer):
        waiting = [chain(layer, 0), chain(layer, 1)]
        while waiting:
            for job in list(waiting):
                if next(job, 0) == 0:
                    waiting.remove(job)
            yield
        yield from post(layer)

    flows = [whole_layer(0), whole_layer(1)]
    turn = 0
    while flows:
        for index, flow in enumerate(list(flows)):
            if len(flows) > 1 and index == 1 and turn < START_ROUND:
                continue
            if next(flow, 0) == 0:
                flows.remove(flow)
        turn += 1

    for sent, copy in drain:
        pl.when(sent)(copy.wait_send)


def per_device(mesh_shape, grads, owners):
    n_dp, n_head = mesh_shape["dp"], mesh_shape["head"]
    _, layers, rank, columns = grads.shape
    x_size = math.isqrt(n_dp // 2)
    z_size, y_size = n_dp // x_size, n_head // 2
    wide = max(TILE, columns * 5 // 8 // TILE * TILE)
    wide_b = columns - wide
    chosen = (owners == lax.axis_index("dp")).astype(F32)
    dma = pltpu.SemaphoreType.DMA

    def slots(first, width):
        second = n_dp // first
        return [
            pltpu.VMEM((layers, first + 1, rank // first, width), BF16),
            pltpu.VMEM((layers, second + 1, rank // n_dp, width), BF16),
        ]

    order = (x_size, z_size, z_size, x_size)
    square = pltpu.VMEM((rank, rank), F32)
    pair = pltpu.VMEM((layers, rank, rank), F32)
    flat = [pltpu.VMEM((layers, rank, w), BF16) for w in (wide, wide_b)]
    scratch = flat + flat + slots(x_size, wide) + slots(z_size, wide_b)
    scratch += [
        pair,
        pltpu.VMEM((layers, rank // 2, rank), F32),
        pltpu.VMEM((layers, y_size, rank // 2, rank), F32),
        pair, square, square, square,
        pltpu.VMEM((rank, rank), BF16),
        pltpu.VMEM((rank, TILE), BF16),
        dma((layers, 2)),
    ]
    scratch += [dma((layers, 2, n)) for n in order] + [dma((layers, n + 1)) for n in order]
    scratch += [dma((layers, 2, n)) for n in order] + [dma((layers, n)) for n in order]
    scratch += [dma((layers, 2)), dma((layers, 2)), dma((layers, y_size)), dma((layers, y_size))]
    vmem = pl.BlockSpec(memory_space=pltpu.VMEM)
    return pl.pallas_call(
        functools.partial(kernel, (z_size, x_size, y_size, rank, wide, wide_b, columns * n_head)),
        out_shape=(
            jax.ShapeDtypeStruct((layers, rank // n_dp, columns), BF16),
            jax.ShapeDtypeStruct((1, rank, columns), BF16),
        ),
        in_specs=[pl.BlockSpec(memory_space=pl.ANY), pl.BlockSpec(memory_space=pltpu.SMEM)],
        out_specs=(vmem, vmem),
        scratch_shapes=scratch,
        compiler_params=pltpu.CompilerParams(
            collective_id=0, has_side_effects=True, vmem_limit_bytes=58 * 1024 * 1024
        ),
    )(grads, chosen)


def solution(mesh):
    in_specs = (P("dp", None, None, "head"), P())
    out_specs = (P(None, "dp", "head"), P("dp", None, "head"))
    return jax.shard_map(
        functools.partial(per_device, dict(mesh.shape)),
        mesh=mesh, in_specs=in_specs, out_specs=out_specs, check_vma=False,
    )
```

time: 609 us -> 305 us (0.50)
  waiting for transfers between devices: 549 us -> 0 us
  Pallas kernels: 0 us -> 296 us
  matrix products: 33.8 us -> 0 us
  between operations: 13.8 us -> 0.64 us
    pallas_call x0 -> x1, Pallas kernels: none -> 296 us  [per_device(): pl.pallas_call(functools.partial(kernel, (z_size, x_size, y_size, rank, w...]
    psum x2 -> x0, waiting for transfers between devices: 269 us -> none  [wide_total(): return lax.psum(gram_part, ('dp', 'head'))]
    reduce_scatter x1 -> x0, waiting for transfers between devices: 156 us -> none  [per_device(): lax.psum_scatter(partial_value.astype(jnp.bfloat16), 'dp', scatter_dimens...]
    all_gather x1 -> x0, waiting for transfers between devices: 124 us -> none  [per_device(): every_layer = lax.all_gather(spread, 'dp', axis=2, tiled=True)]
    dot_general x7 -> x0, matrix products: 33.8 us -> none  [the longest x1 15.3 us: per_device(): jnp.einsum('l,lrc->rc', chosen, every_layer, preferred_element_type=jnp.f...]
    unnamed x6 -> x2, local copies, waits for them, and re-layouts: 0.06 us -> 6.99 us
    dot_general x1 -> x0, local copies, waits for them, and re-layouts: 6.78 us -> none  [per_device(): jnp.einsum('l,lrc->rc', chosen, every_layer, preferred_element_type=jnp.f...]
  transfers between devices with their start and end apart: 4 -> 0, of which waited for: 4 -> 0; matrix products, arithmetic and copies ran while one was open for 0% -> 0% of each run, Pallas kernels for 0% -> 0%
where the time goes in v1:
time: 305 us; the launch traced here: 304 us
  Pallas kernels  296 us (97%)
  local copies, waits for them, and re-layouts  6.99 us (2%)
    pallas_call x1, Pallas kernels, per_device(): pl.pallas_call(functools.partial(kernel, (z_size, x_size, y_size, rank, w...  296 us
    unnamed x2, local copies, waits for them, and re-layouts  6.99 us

profile of v1, /device:TPU:0, one launch (start us, length us, event | category | flops | bytes accessed | tf_op | source)
XLA Modules:
  0.0 304.4 jit_solution(4135182094893903649)
XLA Ops:
  0.6 1.2 compare_convert_fusion.refs_1_
  1.8 295.6 %shard_map.41 = (bf16[2,64,4096]{2,1,0:T(8,128)(2,1)}, bf16[1,512,4096]{2,1,0:T(8,128)(2,1)}) custom-call(bf16[1,2,512,4096]{3,2,1,0:T(8,128)(2,1)} %refs_0_.1, f32[2]{0:T(128)} %compare_convert_fusion.refs_1_), custom_call_target="tpu_custom_call" | custom-call | tf_op jit(solution)/shard_map/pallas_call | solution.py:384
  297.4 2.3 copy.6
  299.7 4.7 %copy.7 = bf16[1,512,4096]{2,1,0:T(8,128)(2,1)} copy(bf16[1,512,4096]{2,1,0:T(8,128)(2,1)} %get-tuple-element.5) | data formatting | bytes 8388608

commit v2 on v1

--- a/solution.py
+++ b/solution.py
@@ -136,7 +136,7 @@
     grads, chosen, updates, owned = take(4)
     acc, fin = take(2), take(2)
     slots_a, slots_b = take(2), take(2)
-    raw, half_in, by_y, full, m0, t0, g1, dmat, outs = take(9)
+    raw, half_in, by_y, full, m0, t0, g1, dmat, outs, right_hi, right_lo = take(11)
     load_sem = take(1)[0]
     rs_send, rs_recv = take(4), take(4)
     ag_send, ag_recv = take(4), take(4)
@@ -213,17 +213,24 @@
             )
 
     def product(left, right, finish):
-        step = 128
+        step = 256
+        value = right[...]
+        right_hi[...] = value.astype(BF16)
+        right_lo[...] = (value - right_hi[...].astype(F32)).astype(BF16)
 
         @pl.loop(0, rank // step)
         def _(index):
             at = pl.ds(pl.multiple_of(index * step, step), step)
-            finish(at, jnp.dot(left[at, :], right[...], precision=lax.Precision.HIGHEST,
-                               preferred_element_type=F32), index * step)
+            block = left[at, :]
+            hi = block.astype(BF16)
+            lo = (block - hi.astype(F32)).astype(BF16)
+            dot = functools.partial(jnp.dot, preferred_element_type=F32)
+            total = dot(hi, right_lo[...]) + dot(lo, right_hi[...]) + dot(hi, right_hi[...])
+            finish(at, total, index * step)
 
     def eye(start):
-        rows = lax.broadcasted_iota(jnp.int32, (128, rank), 0) + start
-        return rows == lax.broadcasted_iota(jnp.int32, (128, rank), 1)
+        rows = lax.broadcasted_iota(jnp.int32, (256, rank), 0) + start
+        return rows == lax.broadcasted_iota(jnp.int32, (256, rank), 1)
 
     def post(layer):
         raw[layer] = jnp.zeros((rank, rank), F32)
@@ -237,7 +244,7 @@
         give.start()
         yield
         give.wait_recv()
-        by_y[layer, y] = raw[layer, mine, :] + half_in[layer]
+        by_y[layer, y] = (raw[layer, mine, :] + half_in[layer]).astype(BF16)
         sends = []
         for step, peer in enumerate(peers):
             copy = remote(by_y.at[layer, y], by_y.at[layer, y], y_send.at[layer, step],
@@ -250,9 +257,9 @@
             source = lax.rem(y + step, y_size)
             remote(by_y.at[layer, source], by_y.at[layer, source], y_send.at[layer, 0],
                    y_recv.at[layer, source], sibling).wait_recv()
-        total = by_y[layer, 0]
+        total = by_y[layer, 0].astype(F32)
         for place in range(1, y_size):
-            total = total + by_y[layer, place]
+            total = total + by_y[layer, place].astype(F32)
         full[layer, mine, :] = total
         share = remote(full.at[layer, mine, :], full.at[layer, mine, :], core_send.at[layer, 1],
                        core_recv.at[layer, 1], sibling)
@@ -371,10 +378,11 @@
     scratch += [
         pair,
         pltpu.VMEM((layers, rank // 2, rank), F32),
-        pltpu.VMEM((layers, y_size, rank // 2, rank), F32),
+        pltpu.VMEM((layers, y_size, rank // 2, rank), BF16),
         pair, square, square, square,
         pltpu.VMEM((rank, rank), BF16),
         pltpu.VMEM((rank, TILE), BF16),
+        pltpu.VMEM((rank, rank), BF16), pltpu.VMEM((rank, rank), BF16),
         dma((layers, 2)),
     ]
     scratch += [dma((layers, 2, n)) for n in order] + [dma((layers, n + 1)) for n in order]

time: 305 us -> 290 us (0.951)
  Pallas kernels: 296 us -> 280 us
    pallas_call x1, Pallas kernels: 296 us -> 280 us  [per_device(): pl.pallas_call(functools.partial(kernel, (z_size, x_size, y_size, rank, w...]
where the time goes in v2:
time: 290 us; the launch traced here: 289 us
  Pallas kernels  280 us (97%)
  local copies, waits for them, and re-layouts  6.99 us (2%)
    pallas_call x1, Pallas kernels, per_device(): pl.pallas_call(functools.partial(kernel, (z_size, x_size, y_size, rank, w...  280 us
    unnamed x2, local copies, waits for them, and re-layouts  6.99 us

profile of v2, /device:TPU:0, one launch (start us, length us, event | category | flops | bytes accessed | tf_op | source)
XLA Modules:
  0.0 289.0 jit_solution(1227786540386205710)
XLA Ops:
  0.6 1.2 compare_convert_fusion.refs_1_
  1.8 280.2 %shard_map.41 = (bf16[2,64,4096]{2,1,0:T(8,128)(2,1)}, bf16[1,512,4096]{2,1,0:T(8,128)(2,1)}) custom-call(bf16[1,2,512,4096]{3,2,1,0:T(8,128)(2,1)} %refs_0_.1, f32[2]{0:T(128)} %compare_convert_fusion.refs_1_), custom_call_target="tpu_custom_call" | custom-call | tf_op jit(solution)/shard_map/pallas_call | solution.py:392
  282.0 2.3 copy.6
  284.3 4.7 %copy.7 = bf16[1,512,4096]{2,1,0:T(8,128)(2,1)} copy(bf16[1,512,4096]{2,1,0:T(8,128)(2,1)} %get-tuple-element.5) | data formatting | bytes 8388608

commit v3 on v2

--- a/solution.py
+++ b/solution.py
@@ -13,7 +13,7 @@
 COEF_C = 2.0315
 EPS = 1e-07
 TILE = 512
-START_ROUND = 5
+START_ROUND = 4
 MESH = pl.DeviceIdType.MESH
 F32 = jnp.float32
 BF16 = jnp.bfloat16
@@ -48,7 +48,7 @@
         return self.device(self.place + 1)
 
 
-def reduce_scatter(line, view, out, rows, slots, send, recv, drain):
+def reduce_scatter(line, view, out, rows, slots, send, recv, drain, pause=0):
     n, i = line.size, line.place
 
     def receive(slot):
@@ -81,6 +81,9 @@
         rightward(n - 1 - step)
         yield
         leftward(step)
+        yield
+
+    for _ in range(pause):
         yield
 
     @pl.when(i == 0)
@@ -191,7 +194,7 @@
         k = 2 * job
         yield from reduce_scatter(
             first, lambda t: a.at[spread_rows(t, big), :], a.at[spread_rows(first.place, big), :], big,
-            slots1.at[layer], rs_send[k].at[layer], rs_recv[k].at[layer], drain,
+            slots1.at[layer], rs_send[k].at[layer], rs_recv[k].at[layer], drain, 3 if layer > 0 and job == 0 else 0,
         )
         yield from reduce_scatter(
             second, lambda t: a.at[small_rows(t), :], f.at[small_rows(second.place), :], small,

time: 290 us -> 293 us (1.010)
  no operation moved by 1% of the time
where the time goes in v3:
time: 293 us; the launch traced here: 289 us
  Pallas kernels  281 us (96%)
  local copies, waits for them, and re-layouts  6.99 us (2%)
    pallas_call x1, Pallas kernels, per_device(): pl.pallas_call(functools.partial(kernel, (z_size, x_size, y_size, rank, w...  281 us
    unnamed x2, local copies, waits for them, and re-layouts  6.99 us

profile of v3, /device:TPU:0, one launch (start us, length us, event | category | flops | bytes accessed | tf_op | source)
XLA Modules:
  0.0 289.3 jit_solution(1692667452498286552)
XLA Ops:
  0.6 1.2 compare_convert_fusion.refs_1_
  1.8 280.5 %shard_map.41 = (bf16[2,64,4096]{2,1,0:T(8,128)(2,1)}, bf16[1,512,4096]{2,1,0:T(8,128)(2,1)}) custom-call(bf16[1,2,512,4096]{3,2,1,0:T(8,128)(2,1)} %refs_0_.1, f32[2]{0:T(128)} %compare_convert_fusion.refs_1_), custom_call_target="tpu_custom_call" | custom-call | tf_op jit(solution)/shard_map/pallas_call | solution.py:395
  282.3 2.3 copy.6
  284.6 4.7 %copy.7 = bf16[1,512,4096]{2,1,0:T(8,128)(2,1)} copy(bf16[1,512,4096]{2,1,0:T(8,128)(2,1)} %get-tuple-element.5) | data formatting | bytes 8388608
